TPU v7x, 32 devices: a whole 2x2x4 slice. The times are simulated.
32 devices in a mesh: groups: 2 (over x), seq: 16 (over z, y, core).
Axes of the slice: x: 2, y: 2, z: 4, core: 2. Of those that a mesh axis runs over, the one named last changes fastest.
Arguments:
- query: bfloat16 [4096, 4096], P(('groups', 'seq')), parts along dimension 0, may hold values from -6 to 6
- key_in: bfloat16 [4096, 4096], P(('groups', 'seq')), parts along dimension 0, may hold values from -6 to 6
- value: bfloat16 [4096, 4096], P(('groups', 'seq')), parts along dimension 0, may hold values from -6 to 6
- q_gain: float32 [4096], replicated, may hold values from 0.25 to 1.75
- k_gain: float32 [4096], replicated, may hold values from 0.25 to 1.75
- tile_list: int32 [32, 16, 3], replicated, may hold values from 0 to 15, as said below
- tile_count: int32 [32, 16], replicated, may hold values from 1 to 3, as said below
Outputs:
- attended: bfloat16 [4096, 4096], P(('groups', 'seq')), parts along dimension 0
There are 2 independent parts, one for each index of `groups`. A program takes and returns all parts, laid end to end along the dimension named above; an argument that names none is the same for every part. Nothing has to cross between parts.
Inputs may be any that keep to these rules, and one draw needn't show every extreme that they name: `tile_list`: the first entry of every list is the query block itself; the used entries of a list are distinct; unused entries also hold block numbers. `tile_count`: some list uses all 3 entries in every draw.
All inputs are finite; a program needn't handle non-finite values.
Results may differ from a plain program's by a relative error of at most 0.0086.
Values may be sent and summed in bfloat16 or wider, within the bound.
A program may use at most 128 MiB of HBM per device.

v0:
```python
import math

import jax
import jax.numpy as jnp
from jax import lax
from jax.sharding import PartitionSpec as P

HEAD_DIM = 128
BLOCK = 128


EPSILON = 1e-06


def rms_scaled(row_data, gain_row):
    values = row_data.astype(jnp.float32)
    power = jnp.mean(values * values, axis=-1, keepdims=True)
    return (values * lax.rsqrt(power + EPSILON) * gain_row).astype(jnp.bfloat16)


def per_device(query, key_in, value, q_gain, k_gain, tile_list, tile_count):
    devices = lax.axis_size("seq")
    tok_rows, row_width = query.shape
    head_dim = HEAD_DIM
    block_rows = BLOCK
    head_count = row_width // head_dim
    replicas = max(1, devices // head_count)
    heads_dev = max(1, head_count // devices)
    group_count = head_count // heads_dev
    slot_count = tile_list.shape[-1]
    blocks = tile_list.shape[1]
    position = lax.axis_index("seq")
    residue = position % replicas
    head_group = position // replicas
    logit_scale = head_dim ** (-0.5)
    q_normed = rms_scaled(query, q_gain)
    k_normed = rms_scaled(key_in, k_gain)

    def whole_rows(row_data):
        split = row_data.reshape(tok_rows, group_count, 1, heads_dev, head_dim)
        spread = jnp.broadcast_to(split, (tok_rows, group_count, replicas, heads_dev, head_dim))
        return spread.transpose(1, 2, 3, 0, 4).reshape(devices, heads_dev, tok_rows, head_dim)

    stacked = jnp.stack([whole_rows(q_normed), whole_rows(k_normed), whole_rows(value)], axis=1)
    received = lax.all_to_all(stacked, "seq", split_axis=0, concat_axis=0, tiled=True)
    full_rows = received.transpose(1, 2, 0, 3, 4).reshape(
        3, heads_dev, devices * tok_rows, head_dim
    )
    own_blocks = blocks // replicas
    query_sets = full_rows[0].reshape(heads_dev, own_blocks, replicas, block_rows, head_dim)
    queries = lax.dynamic_index_in_dim(query_sets, residue, axis=2, keepdims=False)
    queries = queries.reshape(heads_dev * own_blocks, block_rows, head_dim)
    query_block = jnp.arange(own_blocks) * replicas + residue
    head_ids = head_group * heads_dev + jnp.arange(heads_dev)
    item_slots = (
        tile_list[head_ids][:, query_block] + (jnp.arange(heads_dev) * blocks)[:, None, None]
    )
    item_slots = item_slots.reshape(-1, slot_count)
    counts = tile_count[head_ids][:, query_block].reshape(-1)
    key_tiles_all = full_rows[1].reshape(heads_dev * blocks, block_rows, head_dim)
    value_tiles_all = full_rows[2].reshape(heads_dev * blocks, block_rows, head_dim)
    item_count = queries.shape[0]
    per_step = math.gcd(item_count, max(1, 512 // block_rows))

    def padded(q_items, tile_slots, filled):
        gathered_key_tiles = jnp.take(key_tiles_all, tile_slots, axis=0).reshape(
            per_step, slot_count * block_rows, head_dim
        )
        gathered_value_tiles = jnp.take(value_tiles_all, tile_slots, axis=0).reshape(
            per_step, slot_count * block_rows, head_dim
        )
        tile_scores = (
            jnp.einsum(
                "gqd,gkd->gqk", q_items, gathered_key_tiles, preferred_element_type=jnp.float32
            )
            * logit_scale
        )
        is_valid = jnp.repeat(
            jnp.arange(slot_count)[None, :] < filled[:, None], block_rows, axis=1
        )[:, None, :]
        row_max = jnp.max(jnp.where(is_valid, tile_scores, -jnp.inf), axis=-1, keepdims=True)
        weights_f = jnp.where(is_valid, jnp.exp(tile_scores - row_max), 0.0)
        row_total = jnp.sum(weights_f, axis=-1, keepdims=True)
        weighted_values = jnp.einsum(
            "gqk,gkd->gqd",
            weights_f.astype(jnp.bfloat16),
            gathered_value_tiles,
            preferred_element_type=jnp.float32,
        )
        return (weighted_values / row_total).astype(jnp.bfloat16)

    def attend(batch_in):
        q_items, tile_slots, filled = batch_in
        return padded(q_items, tile_slots, filled)

    steps_n = item_count // per_step
    outputs = lax.map(
        attend,
        (
            queries.reshape(steps_n, per_step, block_rows, head_dim),
            item_slots.reshape(steps_n, per_step, slot_count),
            counts.reshape(steps_n, per_step),
        ),
    )
    outputs = outputs.reshape(heads_dev, own_blocks, 1, block_rows, head_dim)
    chosen = (jnp.arange(replicas) == residue).astype(jnp.bfloat16)[None, None, :, None, None]
    placed = (
        (outputs * chosen).reshape(heads_dev, devices, tok_rows, head_dim).transpose(1, 0, 2, 3)
    )
    returned = lax.all_to_all(placed, "seq", split_axis=0, concat_axis=0, tiled=True)
    returned = returned.reshape(group_count, replicas, heads_dev, tok_rows, head_dim)
    combined = jnp.sum(returned.astype(jnp.float32), axis=1).astype(jnp.bfloat16)
    return combined.transpose(2, 0, 1, 3).reshape(tok_rows, row_width)


def solution(mesh):
    return jax.shard_map(
        per_device,
        mesh=mesh,
        in_specs=(
            P(("groups", "seq"), None),
            P(("groups", "seq"), None),
            P(("groups", "seq"), None),
            P(),
            P(),
            P(),
            P(),
        ),
        out_specs=P(("groups", "seq"), None),
        check_vma=False,
    )
```

profile of v0, /device:TPU:0, one launch (start us, length us, event | category | flops | bytes accessed | tf_op | source)
XLA Modules:
  0.0 157.3 jit_solution(16598638640302300269)
XLA Ops:
  0.0 1.7 %copy.38 = bf16[128,4096]{0,1:T(8,128)(2,1)S(1)} copy(bf16[128,4096]{1,0:T(8,128)(2,1)} %param.11) | data formatting | bytes 2097152 | tf_op args[0]
  3.5 2.3 %copy.40 = bf16[128,4096]{0,1:T(8,128)(2,1)} copy(bf16[128,4096]{1,0:T(8,128)(2,1)} %param.13) | data formatting | bytes 2097152 | tf_op args[2]
  7.6 2.8 %copy.41 = bf16[16,3,2,128,128]{4,3,2,1,0:T(8,128)(2,1)} copy(bf16[16,3,2,128,128]{3,4,2,0,1:T(8,128)(2,1)S(1)} %pad_maximum_fusion) | data formatting | bytes 6291456 | tf_op jit(solution)/shard_map/stack | solution.py:44
  10.4 7.5 %all-to-all-start = ((bf16[16,3,2,128,128]{4,3,2,1,0:T(8,128)(2,1)}), bf16[16,3,2,128,128]{4,3,2,1,0:T(8,128)(2,1)S(1)}, u32[]{:S(2)}, u32[]{:S(2)}) async-start(bf16[16,3,2,128,128]{4,3,2,1,0:T(8,128)(2,1)} %copy.41), calls=%async_computation | async-start | bytes 6291456 | tf_op jit(solution)/shard_map/all_to_all | solution.py:45
  21.2 56.1 %all-to-all-done = bf16[16,3,2,128,128]{4,3,2,1,0:T(8,128)(2,1)S(1)} async-done(((bf16[16,3,2,128,128]{4,3,2,1,0:T(8,128)(2,1)}), bf16[16,3,2,128,128]{4,3,2,1,0:T(8,128)(2,1)S(1)}, u32[]{:S(2)}, u32[]{:S(2)}) %all-to-all-start) | async-done | bytes 3145760 | tf_op jit(solution)/shard_map/all_to_all | solution.py:45
  77.5 1.3 fusion.31
  78.8 33.9 %while.10 = (s32[]{:T(128)}, bf16[8,4,128,128]{3,2,1,0:T(8,128)(2,1)}, s32[8,4]{1,0:T(8,128)S(1)}, bf16[8,4,128,128]{3,2,1,0:T(8,128)(2,1)}, s32[8,4,3]{1,0,2:T(...) while((s32[]{:T(128)}, ...), condition=%wide.region_5.7_spmd, body=%wide.region_2.6_spmd.sunk | while | flops 102959480 | bytes 7356157 | solution.py:97
  80.4 1.2 convolution_multiply_fusion.2
  82.0 1.0 fusion.49
  84.7 1.2 convolution_multiply_fusion.2
  86.3 1.0 fusion.49
  88.9 1.2 convolution_multiply_fusion.2
  90.5 1.0 fusion.49
  93.2 1.2 convolution_multiply_fusion.2
  94.8 1.0 fusion.49
  97.4 1.2 convolution_multiply_fusion.2
  99.0 1.0 fusion.49
  101.6 1.2 convolution_multiply_fusion.2
  105.9 1.2 convolution_multiply_fusion.2
  107.5 1.0 fusion.49
  110.1 1.2 convolution_multiply_fusion.2
  112.8 2.3 %copy.47 = bf16[16,2,128,128]{3,1,2,0:T(2,128)(2,1)S(1)} copy(bf16[16,2,128,128]{3,2,0,1:T(8,128)(2,1)} %bitcast.84) | data formatting | bytes 2097152 | tf_op jit(solution)/shard_map/transpose | solution.py:108
  115.1 40.1 %all_to_all.10 = bf16[16,2,128,128]{3,1,2,0:T(2,128)(2,1)S(1)} all-to-all(bf16[16,2,128,128]{3,1,2,0:T(2,128)(2,1)S(1)} %copy.47), channel_id=1, replica_groups=mesh['groups'=2,'seq'=16] {'seq'}, dimensions={0} | all-to-all | bytes 2097152 | tf_op jit(solution)/shard_map/all_to_all | solution.py:110
  156.0 1.3 copy.49
  (149 shorter events, 25.6 us)
Async XLA Ops:
  0.0 2.3 %copy-start.1 = (bf16[128,4096]{1,0:T(8,128)(2,1)S(1)}, bf16[128,4096]{1,0:T(8,128)(2,1)}, u32[]{:S(2)}) copy-start(bf16[128,4096]{1,0:T(8,128)(2,1)} %param.12) | copy-start | bytes 3145732
  2.9 2.9 %copy-start.3 = (f32[4096]{0:T(1024)S(1)}, f32[4096]{0:T(1024)}, u32[]{:S(2)}) copy-start(f32[4096]{0:T(1024)} %param.14) | copy-start | bytes 49156
  3.5 3.0 %copy-start.4 = (f32[4096]{0:T(1024)S(1)}, f32[4096]{0:T(1024)}, u32[]{:S(2)}) copy-start(f32[4096]{0:T(1024)} %param.15) | copy-start | bytes 49156
  5.8 1.4 copy-start
  10.4 7.5 %copy-start.2 = (s32[32,16,3]{0,1,2:T(8,128)S(1)}, s32[32,16,3]{0,1,2:T(8,128)}, u32[]{:S(2)}) copy-start(s32[32,16,3]{0,1,2:T(8,128)} %param.16) | copy-start | bytes 18436
  10.4 9.3 %copy-start.5 = (s32[32,16]{0,1:T(8,128)S(1)}, s32[32,16]{0,1:T(8,128)}, u32[]{:S(2)}) copy-start(s32[32,16]{0,1:T(8,128)} %param.17) | copy-start | bytes 6148
  10.4 66.9 %all-to-all-start = ((bf16[16,3,2,128,128]{4,3,2,1,0:T(8,128)(2,1)}), bf16[16,3,2,128,128]{4,3,2,1,0:T(8,128)(2,1)S(1)}, u32[]{:S(2)}, u32[]{:S(2)}) async-start(bf16[16,3,2,128,128]{4,3,2,1,0:T(8,128)(2,1)} %copy.41), calls=%async_computation | async-start | bytes 6291456 | tf_op jit(solution)/shard_map/all_to_all | solution.py:45
where the time goes:
time: 158 us; the launch traced here: 157 us
  waiting for transfers between devices  56.1 us (36%)
  blocking collectives  40.1 us (25%)
  local copies, waits for them, and re-layouts  28.7 us (18%)
  matrix products  17.7 us (11%)
  starting transfers between devices  7.52 us (5%)
  other arithmetic  6.64 us (4%)
    all_to_all x1, waiting for transfers between devices, per_device(): lax.all_to_all(stacked, 'seq', split_axis=0, concat_axis=0, tiled=True)  56.1 us
    all_to_all x1, blocking collectives, per_device(): lax.all_to_all(placed, 'seq', split_axis=0, concat_axis=0, tiled=True)  40.1 us
    dot_general x8, matrix products, padded(): jnp.einsum('gqd,gkd->gqk', q_items, gathered_key_tiles, preferred_element...  9.69 us
    dot_general x8, matrix products, padded(): jnp.einsum('gqk,gkd->gqd', weights_f.astype(jnp.bfloat16), gathered_value...  8.01 us
    all_to_all x1, starting transfers between devices, per_device(): lax.all_to_all(stacked, 'seq', split_axis=0, concat_axis=0, tiled=True)  7.52 us
    gather x8, local copies, waits for them, and re-layouts, padded(): jnp.take(value_tiles_all, tile_slots, axis=0)  4.98 us
    gather x8, local copies, waits for them, and re-layouts, padded(): jnp.take(key_tiles_all, tile_slots, axis=0)  4.97 us
    unnamed x17, local copies, waits for them, and re-layouts  4.82 us
  transfers between devices with their start and end apart: 1, of which 1 were waited for; matrix products, arithmetic and copies ran while one was open for 2% of the time, Pallas kernels for 0%

commit v1 on v0

--- a/solution.py
+++ b/solution.py
@@ -1,15 +1,268 @@
+import functools
 import math
 
 import jax
 import jax.numpy as jnp
 from jax import lax
+from jax.experimental import pallas as pl
+from jax.experimental.pallas import tpu as pltpu
 from jax.sharding import PartitionSpec as P
 
 HEAD_DIM = 128
 BLOCK = 128
-
-
+ROW_TILE = 16
 EPSILON = 1e-06
+MESH = pl.DeviceIdType.MESH
+
+
+def attention_kernel(
+    n,
+    heads_dev,
+    slot_count,
+    list_hbm,
+    count_hbm,
+    q_gain,
+    k_gain,
+    q_hbm,
+    k_hbm,
+    v_hbm,
+    out,
+    list_smem,
+    count_smem,
+    q_in,
+    k_in,
+    q_send,
+    k_send,
+    q_all,
+    k_all,
+    v_all,
+    o_send,
+    load_sem,
+    own_sem,
+    send_sem,
+    recv_sem,
+    back_send_sem,
+    back_recv_sem,
+):
+    me = lax.axis_index("seq")
+    heads = n * heads_dev
+    width = heads * HEAD_DIM
+    logit_scale = HEAD_DIM ** (-0.5)
+    my_heads = pl.ds(me * heads_dev, heads_dev)
+
+    loads = [
+        pltpu.make_async_copy(q_hbm, q_in, load_sem.at[0]),
+        pltpu.make_async_copy(k_hbm, k_in, load_sem.at[1]),
+        pltpu.make_async_copy(list_hbm.at[my_heads], list_smem, load_sem.at[2]),
+        pltpu.make_async_copy(count_hbm.at[my_heads], count_smem, load_sem.at[3]),
+    ]
+    for load in loads:
+        load.start()
+
+    barrier = pltpu.get_barrier_semaphore()
+
+    def greet(i, carry):
+        peer = lax.rem(me + 1 + i, n)
+        pl.semaphore_signal(barrier, inc=1, device_id={"seq": peer}, device_id_type=MESH)
+        return carry
+
+    lax.fori_loop(0, n - 1, greet, 0)
+    pl.semaphore_wait(barrier, n - 1)
+
+    def partner(i):
+        return lax.rem(me + 1 + lax.rem(n // 2 - 1 + i, n - 1), n)
+
+    def v_columns(head):
+        return v_hbm.at[:, pl.ds(pl.multiple_of(head * HEAD_DIM, HEAD_DIM), HEAD_DIM)]
+
+    def out_columns(head):
+        return out.at[:, pl.ds(pl.multiple_of(head * HEAD_DIM, HEAD_DIM), HEAD_DIM)]
+
+    sources = (
+        (v_columns, v_all),
+        (lambda head: q_send.at[head], q_all),
+        (lambda head: k_send.at[head], k_all),
+    )
+
+    def own_copy(kind, h):
+        source, landing = sources[kind]
+        return pltpu.make_async_copy(
+            source(me * heads_dev + h), landing[h].at[me], own_sem.at[kind, h]
+        )
+
+    def spread(kind, h):
+        source, landing = sources[kind]
+
+        def body(i, carry):
+            peer = partner(i)
+            pltpu.make_async_remote_copy(
+                src_ref=source(peer * heads_dev + h),
+                dst_ref=landing[h].at[me],
+                send_sem=send_sem.at[kind, h],
+                recv_sem=recv_sem.at[kind, h],
+                device_id={"seq": peer},
+                device_id_type=MESH,
+            ).start()
+            return carry
+
+        lax.fori_loop(0, n - 1, body, 0)
+        own_copy(kind, h).start()
+
+    def normalise(source, gain, target):
+        def rows_step(i, carry):
+            rows = pl.ds(pl.multiple_of(i * ROW_TILE, ROW_TILE), ROW_TILE)
+            squares = jnp.zeros((ROW_TILE, HEAD_DIM), jnp.float32)
+            for head in range(heads):
+                part = source[rows, head * HEAD_DIM : (head + 1) * HEAD_DIM].astype(jnp.float32)
+                squares = squares + part * part
+            power = jnp.sum(squares, axis=-1, keepdims=True) / width
+            scale = lax.rsqrt(power + EPSILON)
+            for head in range(heads):
+                columns = slice(head * HEAD_DIM, (head + 1) * HEAD_DIM)
+                part = source[rows, columns].astype(jnp.float32)
+                target[head, rows, :] = (part * scale * gain[:, columns]).astype(jnp.bfloat16)
+            return carry
+
+        lax.fori_loop(0, BLOCK // ROW_TILE, rows_step, 0)
+
+    spread(0, 0)
+    loads[0].wait()
+    normalise(q_in, q_gain, q_send)
+    spread(1, 0)
+    loads[1].wait()
+    normalise(k_in, k_gain, k_send)
+    spread(2, 0)
+    for h in range(1, heads_dev):
+        for kind in range(3):
+            spread(kind, h)
+    loads[2].wait()
+    loads[3].wait()
+
+    def landed(buffer, semaphore):
+        others = buffer.at[pl.ds(0, n - 1)]
+        pltpu.make_async_copy(others, others, semaphore).wait()
+
+    def attend(h, block):
+        filled = count_smem[h, block]
+        queries = q_all[h][block]
+        scores = []
+        for slot in range(slot_count):
+            tile = list_smem[h, block, slot]
+            tile_scores = (
+                lax.dot_general(
+                    queries,
+                    k_all[h][tile],
+                    (((1,), (1,)), ((), ())),
+                    preferred_element_type=jnp.float32,
+                )
+                * logit_scale
+            )
+            if slot > 0:
+                tile_scores = jnp.where(
+                    jnp.full(tile_scores.shape, filled, jnp.int32) > slot, tile_scores, -jnp.inf
+                )
+            scores.append(tile_scores)
+        row_max = jnp.max(functools.reduce(jnp.maximum, scores), axis=-1, keepdims=True)
+        weights = [jnp.exp(tile_scores - row_max) for tile_scores in scores]
+        row_total = jnp.sum(functools.reduce(jnp.add, weights), axis=-1, keepdims=True)
+        total = None
+        for slot in range(slot_count):
+            tile = list_smem[h, block, slot]
+            product = jnp.dot(
+                weights[slot].astype(jnp.bfloat16),
+                v_all[h][tile],
+                preferred_element_type=jnp.float32,
+            )
+            total = product if total is None else total + product
+        return (total / row_total).astype(jnp.bfloat16)
+
+    for h in range(heads_dev):
+        for kind in range(3):
+            own_copy(kind, h).wait()
+            landed(sources[kind][1][h], recv_sem.at[kind, h])
+
+        def item(i, carry):
+            block = partner(i)
+            o_send[h, block] = attend(h, block)
+            pltpu.make_async_remote_copy(
+                src_ref=o_send.at[h, block],
+                dst_ref=out_columns(me * heads_dev + h),
+                send_sem=back_send_sem.at[h],
+                recv_sem=back_recv_sem.at[h],
+                device_id={"seq": block},
+                device_id_type=MESH,
+            ).start()
+            return carry
+
+        lax.fori_loop(0, n - 1, item, 0, unroll=UNROLL)
+        o_send[h, me] = attend(h, me)
+        pltpu.make_async_copy(
+            o_send.at[h, me], out_columns(me * heads_dev + h), own_sem.at[3, h]
+        ).start()
+
+    for h in range(heads_dev):
+        pltpu.make_async_copy(
+            o_send.at[h, me], out_columns(me * heads_dev + h), own_sem.at[3, h]
+        ).wait()
+        landed(o_send.at[h], back_recv_sem.at[h])
+        landed(o_send.at[h], back_send_sem.at[h])
+        for kind in range(3):
+            landed(sources[kind][1][h], send_sem.at[kind, h])
+
+
+UNROLL = 3
+
+
+def fused(query, key_in, value, q_gain, k_gain, tile_list, tile_count):
+    n = lax.axis_size("seq")
+    tok_rows, row_width = query.shape
+    head_count = row_width // HEAD_DIM
+    heads_dev = head_count // n
+    slot_count = tile_list.shape[-1]
+    blocks = tile_list.shape[1]
+    any_space = pl.BlockSpec(memory_space=pl.ANY)
+    in_vmem = pl.BlockSpec(memory_space=pltpu.VMEM)
+    landing = (pltpu.VMEM((n, BLOCK, HEAD_DIM), jnp.bfloat16),) * heads_dev
+    return pl.pallas_call(
+        functools.partial(attention_kernel, n, heads_dev, slot_count),
+        out_shape=jax.ShapeDtypeStruct((tok_rows, row_width), jnp.bfloat16),
+        in_specs=[any_space, any_space, in_vmem, in_vmem, any_space, any_space, any_space],
+        out_specs=any_space,
+        scratch_shapes=[
+            pltpu.SMEM((heads_dev, blocks, slot_count), jnp.int32),
+            pltpu.SMEM((heads_dev, blocks), jnp.int32),
+            pltpu.VMEM((tok_rows, row_width), jnp.bfloat16),
+            pltpu.VMEM((tok_rows, row_width), jnp.bfloat16),
+            pltpu.VMEM((head_count, BLOCK, HEAD_DIM), jnp.bfloat16),
+            pltpu.VMEM((head_count, BLOCK, HEAD_DIM), jnp.bfloat16),
+            landing,
+            landing,
+            landing,
+            pltpu.VMEM((heads_dev, n, BLOCK, HEAD_DIM), jnp.bfloat16),
+            pltpu.SemaphoreType.DMA((4,)),
+            pltpu.SemaphoreType.DMA((4, heads_dev)),
+            pltpu.SemaphoreType.DMA((3, heads_dev)),
+            pltpu.SemaphoreType.DMA((3, heads_dev)),
+            pltpu.SemaphoreType.DMA((heads_dev,)),
+            pltpu.SemaphoreType.DMA((heads_dev,)),
+        ],
+        compiler_params=pltpu.CompilerParams(
+            collective_id=0, has_side_effects=True, vmem_limit_bytes=48 * 1024 * 1024
+        ),
+        cost_estimate=pl.CostEstimate(
+            flops=4 * heads_dev * n * slot_count * BLOCK * BLOCK * HEAD_DIM,
+            bytes_accessed=8 * tok_rows * row_width,
+            transcendentals=heads_dev * n * slot_count * BLOCK * BLOCK,
+        ),
+    )(
+        tile_list,
+        tile_count,
+        q_gain.reshape(1, row_width),
+        k_gain.reshape(1, row_width),
+        query,
+        key_in,
+        value,
+    )
 
 
 def rms_scaled(row_data, gain_row):
@@ -18,7 +271,7 @@
     return (values * lax.rsqrt(power + EPSILON) * gain_row).astype(jnp.bfloat16)
 
 
-def per_device(query, key_in, value, q_gain, k_gain, tile_list, tile_count):
+def exchanged(query, key_in, value, q_gain, k_gain, tile_list, tile_count):
     devices = lax.axis_size("seq")
     tok_rows, row_width = query.shape
     head_dim = HEAD_DIM
@@ -113,6 +366,16 @@
     return combined.transpose(2, 0, 1, 3).reshape(tok_rows, row_width)
 
 
+def per_device(query, key_in, value, q_gain, k_gain, tile_list, tile_count):
+    devices = lax.axis_size("seq")
+    tok_rows, row_width = query.shape
+    head_count = row_width // HEAD_DIM
+    one_block = tok_rows == BLOCK and tile_list.shape[1] == devices
+    if devices > 1 and head_count % devices == 0 and one_block:
+        return fused(query, key_in, value, q_gain, k_gain, tile_list, tile_count)
+    return exchanged(query, key_in, value, q_gain, k_gain, tile_list, tile_count)
+
+
 def solution(mesh):
     return jax.shard_map(
         per_device,

time: 158 us -> 104 us (0.66)
  Pallas kernels: 0 us -> 97.9 us
  waiting for transfers between devices: 56.1 us -> 0 us
  blocking collectives: 40.1 us -> 0 us
  local copies, waits for them, and re-layouts: 28.7 us -> 6.15 us
  matrix products: 17.7 us -> 0 us
  starting transfers between devices: 7.52 us -> 0 us
  other arithmetic: 6.64 us -> 0 us
    pallas_call x0 -> x1, Pallas kernels: none -> 97.9 us  [fused(): pl.pallas_call(functools.partial(attention_kernel, n, heads_dev, slot_cou...]
    all_to_all x1 -> x0, waiting for transfers between devices: 56.1 us -> none  [per_device(): lax.all_to_all(stacked, 'seq', split_axis=0, concat_axis=0, tiled=True)]
    all_to_all x1 -> x0, blocking collectives: 40.1 us -> none  [per_device(): lax.all_to_all(placed, 'seq', split_axis=0, concat_axis=0, tiled=True)]
    dot_general x16 -> x0, matrix products: 17.7 us -> none  [the longest x8 9.69 us: padded(): jnp.einsum('gqd,gkd->gqk', q_items, gathered_key_tiles, preferred_element...]
    gather x25 -> x0, local copies, waits for them, and re-layouts: 12.7 us -> none  [the longest x8 4.98 us: padded(): jnp.take(value_tiles_all, tile_slots, axis=0)]
    all_to_all x1 -> x0, starting transfers between devices: 7.52 us -> none  [per_device(): lax.all_to_all(stacked, 'seq', split_axis=0, concat_axis=0, tiled=True)]
    another operation x2 -> x0, local copies, waits for them, and re-layouts: 2.89 us -> none  [the longest x1 2.81 us: per_device(): jnp.stack([whole_rows(q_normed), whole_rows(k_normed), whole_rows(value)]...]
    sub x8 -> x0, other arithmetic: 2.35 us -> none  [padded(): weights_f = jnp.where(is_valid, jnp.exp(tile_scores - row_max), 0.0)]
  transfers between devices with their start and end apart: 1 -> 0, of which waited for: 1 -> 0; matrix products, arithmetic and copies ran while one was open for 2% -> 0% of each run, Pallas kernels for 0% -> 0%
where the time goes in v1:
time: 104 us
  Pallas kernels  97.9 us (94%)
  local copies, waits for them, and re-layouts  6.15 us (6%)
    pallas_call x1, Pallas kernels, fused(): pl.pallas_call(functools.partial(attention_kernel, n, heads_dev, slot_cou...  97.9 us
    unnamed x15, local copies, waits for them, and re-layouts  6.15 us

profile of v1, /device:TPU:0, one launch (start us, length us, event | category | flops | bytes accessed | tf_op | source)
XLA Modules:
  0.0 104.1 jit_solution(1605438955301036524)
XLA Ops:
  0.0 0.0 copy-start.5
  0.0 0.8 copy.9.count_hbm
  0.8 0.0 copy-done.5
  0.8 0.0 copy-start.3
  0.8 0.0 copy-start.4
  0.8 0.2 copy.8.list_hbm
  1.0 0.5 copy-done.3
  1.5 0.0 copy-done.4
  1.5 0.0 copy-start
  1.5 1.2 %copy-done = bf16[128,4096]{1,0:T(8,128)(2,1)S(1)} copy-done((bf16[128,4096]{1,0:T(8,128)(2,1)S(1)}, bf16[128,4096]{1,0:T(8,128)(2,1)}, u32[]{:S(2)}) %copy-start) | copy-done | bytes 1048600
  2.7 0.0 copy-start.1
  2.7 1.2 %copy-done.1 = bf16[128,4096]{1,0:T(8,128)(2,1)S(1)} copy-done((bf16[128,4096]{1,0:T(8,128)(2,1)S(1)}, bf16[128,4096]{1,0:T(8,128)(2,1)}, u32[]{:S(2)}) %copy-start.1) | copy-done | bytes 1048600
  4.0 0.0 copy-start.2
  4.0 1.2 %copy-done.2 = bf16[128,4096]{1,0:T(8,128)(2,1)S(1)} copy-done((bf16[128,4096]{1,0:T(8,128)(2,1)S(1)}, bf16[128,4096]{1,0:T(8,128)(2,1)}, u32[]{:S(2)}) %copy-start.2) | copy-done | bytes 1048600
  5.2 97.9 %shard_map.73 = bf16[128,4096]{1,0:T(8,128)(2,1)S(1)} custom-call(s32[32,16,3]{2,1,0:T(8,128)S(1)} %copy.8.list_hbm, s32[32,16]{1,0:T(8,128)S(1)} %copy.9.count_hbm, f32[1,4096]{1,0:T(1,128)S(1)} %bitcast.2, f32[1,4096]{1,0:T(1,128)S(1)} %bitcast.3, bf16[128,4096]{1,0:T(8,128)(2,1)S(1)} %copy-done, bf16[128,4096]{1,0:T(8,128)(2,1)S(1)} %copy-done.1, ...), custom_call_target="tpu_custom_call" | custom-call | flops 805306368 | bytes 4194304 | tf_op jit(solution)/shard_map/pallas_call | solution.py:226
  103.1 1.0 copy.11
Async XLA Ops:
  0.0 0.8 copy-start.5
  0.8 0.7 copy-start.3
  0.8 0.7 copy-start.4
  1.5 1.2 %copy-start = (bf16[128,4096]{1,0:T(8,128)(2,1)S(1)}, bf16[128,4096]{1,0:T(8,128)(2,1)}, u32[]{:S(2)}) copy-start(bf16[128,4096]{1,0:T(8,128)(2,1)} %q_hbm.1) | copy-start | bytes 3145732
  2.7 1.2 %copy-start.1 = (bf16[128,4096]{1,0:T(8,128)(2,1)S(1)}, bf16[128,4096]{1,0:T(8,128)(2,1)}, u32[]{:S(2)}) copy-start(bf16[128,4096]{1,0:T(8,128)(2,1)} %k_hbm.1) | copy-start | bytes 3145732
  4.0 1.2 %copy-start.2 = (bf16[128,4096]{1,0:T(8,128)(2,1)S(1)}, bf16[128,4096]{1,0:T(8,128)(2,1)}, u32[]{:S(2)}) copy-start(bf16[128,4096]{1,0:T(8,128)(2,1)} %v_hbm.1) | copy-start | bytes 3145732

commit v2 on v1

--- a/solution.py
+++ b/solution.py
@@ -21,14 +21,16 @@
     slot_count,
     list_hbm,
     count_hbm,
-    q_gain,
-    k_gain,
+    q_gain_hbm,
+    k_gain_hbm,
     q_hbm,
     k_hbm,
     v_hbm,
     out,
     list_smem,
     count_smem,
+    q_gain,
+    k_gain,
     q_in,
     k_in,
     q_send,
@@ -48,13 +50,14 @@
     heads = n * heads_dev
     width = heads * HEAD_DIM
     logit_scale = HEAD_DIM ** (-0.5)
-    my_heads = pl.ds(me * heads_dev, heads_dev)
 
     loads = [
         pltpu.make_async_copy(q_hbm, q_in, load_sem.at[0]),
-        pltpu.make_async_copy(k_hbm, k_in, load_sem.at[1]),
-        pltpu.make_async_copy(list_hbm.at[my_heads], list_smem, load_sem.at[2]),
-        pltpu.make_async_copy(count_hbm.at[my_heads], count_smem, load_sem.at[3]),
+        pltpu.make_async_copy(q_gain_hbm, q_gain, load_sem.at[1]),
+        pltpu.make_async_copy(k_hbm, k_in, load_sem.at[2]),
+        pltpu.make_async_copy(k_gain_hbm, k_gain, load_sem.at[3]),
+        pltpu.make_async_copy(list_hbm, list_smem, load_sem.at[4]),
+        pltpu.make_async_copy(count_hbm, count_smem, load_sem.at[5]),
     ]
     for load in loads:
         load.start()
@@ -127,27 +130,29 @@
 
     spread(0, 0)
     loads[0].wait()
+    loads[1].wait()
     normalise(q_in, q_gain, q_send)
     spread(1, 0)
-    loads[1].wait()
+    loads[2].wait()
+    loads[3].wait()
     normalise(k_in, k_gain, k_send)
     spread(2, 0)
     for h in range(1, heads_dev):
         for kind in range(3):
             spread(kind, h)
-    loads[2].wait()
-    loads[3].wait()
+    loads[4].wait()
+    loads[5].wait()
 
     def landed(buffer, semaphore):
         others = buffer.at[pl.ds(0, n - 1)]
         pltpu.make_async_copy(others, others, semaphore).wait()
 
     def attend(h, block):
-        filled = count_smem[h, block]
+        filled = count_smem[block, me * heads_dev + h]
         queries = q_all[h][block]
         scores = []
         for slot in range(slot_count):
-            tile = list_smem[h, block, slot]
+            tile = list_smem[slot, block, me * heads_dev + h]
             tile_scores = (
                 lax.dot_general(
                     queries,
@@ -167,7 +172,7 @@
         row_total = jnp.sum(functools.reduce(jnp.add, weights), axis=-1, keepdims=True)
         total = None
         for slot in range(slot_count):
-            tile = list_smem[h, block, slot]
+            tile = list_smem[slot, block, me * heads_dev + h]
             product = jnp.dot(
                 weights[slot].astype(jnp.bfloat16),
                 v_all[h][tile],
@@ -176,6 +181,22 @@
             total = product if total is None else total + product
         return (total / row_total).astype(jnp.bfloat16)
 
+    def returned(h, block):
+        return pltpu.make_async_remote_copy(
+            src_ref=o_send.at[h, block],
+            dst_ref=out_columns(me * heads_dev + h),
+            send_sem=back_send_sem.at[h],
+            recv_sem=back_recv_sem.at[h],
+            device_id={"seq": block},
+            device_id_type=MESH,
+        )
+
+    def kept(h):
+        return pltpu.make_async_copy(
+            o_send.at[h, me], out_columns(me * heads_dev + h), own_sem.at[3, h]
+        )
+
+    last = heads_dev - 1
     for h in range(heads_dev):
         for kind in range(3):
             own_copy(kind, h).wait()
@@ -184,30 +205,31 @@
         def item(i, carry):
             block = partner(i)
             o_send[h, block] = attend(h, block)
-            pltpu.make_async_remote_copy(
-                src_ref=o_send.at[h, block],
-                dst_ref=out_columns(me * heads_dev + h),
-                send_sem=back_send_sem.at[h],
-                recv_sem=back_recv_sem.at[h],
-                device_id={"seq": block},
-                device_id_type=MESH,
-            ).start()
+            if h == last:
+                returned(h, block).start()
             return carry
 
         lax.fori_loop(0, n - 1, item, 0, unroll=UNROLL)
         o_send[h, me] = attend(h, me)
-        pltpu.make_async_copy(
-            o_send.at[h, me], out_columns(me * heads_dev + h), own_sem.at[3, h]
-        ).start()
+        kept(h).start()
+        if h == last - 1:
+            for kind in range(3):
+                landed(sources[kind][1][last], send_sem.at[kind, last])
+
+            def give_back(i, carry):
+                for done in range(last):
+                    returned(done, partner(i)).start()
+                return carry
+
+            lax.fori_loop(0, n - 1, give_back, 0)
 
     for h in range(heads_dev):
-        pltpu.make_async_copy(
-            o_send.at[h, me], out_columns(me * heads_dev + h), own_sem.at[3, h]
-        ).wait()
+        kept(h).wait()
         landed(o_send.at[h], back_recv_sem.at[h])
         landed(o_send.at[h], back_send_sem.at[h])
-        for kind in range(3):
-            landed(sources[kind][1][h], send_sem.at[kind, h])
+        if h < last or last == 0:
+            for kind in range(3):
+                landed(sources[kind][1][h], send_sem.at[kind, h])
 
 
 UNROLL = 3
@@ -221,16 +243,17 @@
     slot_count = tile_list.shape[-1]
     blocks = tile_list.shape[1]
     any_space = pl.BlockSpec(memory_space=pl.ANY)
-    in_vmem = pl.BlockSpec(memory_space=pltpu.VMEM)
     landing = (pltpu.VMEM((n, BLOCK, HEAD_DIM), jnp.bfloat16),) * heads_dev
     return pl.pallas_call(
         functools.partial(attention_kernel, n, heads_dev, slot_count),
         out_shape=jax.ShapeDtypeStruct((tok_rows, row_width), jnp.bfloat16),
-        in_specs=[any_space, any_space, in_vmem, in_vmem, any_space, any_space, any_space],
+        in_specs=[any_space] * 7,
         out_specs=any_space,
         scratch_shapes=[
-            pltpu.SMEM((heads_dev, blocks, slot_count), jnp.int32),
-            pltpu.SMEM((heads_dev, blocks), jnp.int32),
+            pltpu.SMEM((slot_count, blocks, head_count), jnp.int32),
+            pltpu.SMEM((blocks, head_count), jnp.int32),
+            pltpu.VMEM((1, row_width), jnp.float32),
+            pltpu.VMEM((1, row_width), jnp.float32),
             pltpu.VMEM((tok_rows, row_width), jnp.bfloat16),
             pltpu.VMEM((tok_rows, row_width), jnp.bfloat16),
             pltpu.VMEM((head_count, BLOCK, HEAD_DIM), jnp.bfloat16),
@@ -239,7 +262,7 @@
             landing,
             landing,
             pltpu.VMEM((heads_dev, n, BLOCK, HEAD_DIM), jnp.bfloat16),
-            pltpu.SemaphoreType.DMA((4,)),
+            pltpu.SemaphoreType.DMA((6,)),
             pltpu.SemaphoreType.DMA((4, heads_dev)),
             pltpu.SemaphoreType.DMA((3, heads_dev)),
             pltpu.SemaphoreType.DMA((3, heads_dev)),
@@ -247,7 +270,7 @@
             pltpu.SemaphoreType.DMA((heads_dev,)),
         ],
         compiler_params=pltpu.CompilerParams(
-            collective_id=0, has_side_effects=True, vmem_limit_bytes=48 * 1024 * 1024
+            collective_id=0, has_side_effects=True, vmem_limit_bytes=60 * 1024 * 1024
         ),
         cost_estimate=pl.CostEstimate(
             flops=4 * heads_dev * n * slot_count * BLOCK * BLOCK * HEAD_DIM,
@@ -255,8 +278,8 @@
             transcendentals=heads_dev * n * slot_count * BLOCK * BLOCK,
         ),
     )(
-        tile_list,
-        tile_count,
+        tile_list.transpose(2, 1, 0),
+        tile_count.T,
         q_gain.reshape(1, row_width),
         k_gain.reshape(1, row_width),
         query,

time: 104 us -> 100 us (0.962)
  local copies, waits for them, and re-layouts: 6.15 us -> 2.29 us
    unnamed x15 -> x1, local copies, waits for them, and re-layouts: 6.15 us -> 2.29 us
where the time goes in v2:
time: 100 us
  Pallas kernels  98 us (98%)
  local copies, waits for them, and re-layouts  2.29 us (2%)
    pallas_call x1, Pallas kernels, fused(): pl.pallas_call(functools.partial(attention_kernel, n, heads_dev, slot_cou...  98 us
    unnamed x1, local copies, waits for them, and re-layouts  2.29 us

profile of v2, /device:TPU:0, one launch (start us, length us, event | category | flops | bytes accessed | tf_op | source)
XLA Modules:
  0.0 100.3 jit_solution(4175427103631857505)
XLA Ops:
  0.0 98.0 %shard_map.73 = bf16[128,4096]{1,0:T(8,128)(2,1)} custom-call(s32[3,16,32]{2,1,0:T(8,128)} %bitcast.4, s32[16,32]{1,0:T(8,128)} %bitcast.7, f32[1,4096]{1,0:T(1,128)} %bitcast.5, f32[1,4096]{1,0:T(1,128)} %bitcast.6, bf16[128,4096]{1,0:T(8,128)(2,1)} %q_hbm.1, bf16[128,4096]{1,0:T(8,128)(2,1)} %k_hbm.1, bf16[128,4096]{1,0:T(8,128)(2,1)} %v_hbm.1), custom_call_target="tpu_custom_call" | custom-call | flops 805306368 | bytes 4194304 | tf_op jit(solution)/shard_map/pallas_call | solution.py:247
  98.0 2.3 %copy.9 = bf16[128,4096]{1,0:T(8,128)(2,1)} copy(bf16[128,4096]{1,0:T(8,128)(2,1)} %shard_map.73) | data formatting | bytes 2097152

commit v3 on v2

--- a/solution.py
+++ b/solution.py
@@ -270,7 +270,7 @@
             pltpu.SemaphoreType.DMA((heads_dev,)),
         ],
         compiler_params=pltpu.CompilerParams(
-            collective_id=0, has_side_effects=True, vmem_limit_bytes=60 * 1024 * 1024
+            collective_id=0, has_side_effects=True, vmem_limit_bytes=40 * 1024 * 1024
         ),
         cost_estimate=pl.CostEstimate(
             flops=4 * heads_dev * n * slot_count * BLOCK * BLOCK * HEAD_DIM,
@@ -278,13 +278,18 @@
             transcendentals=heads_dev * n * slot_count * BLOCK * BLOCK,
         ),
     )(
-        tile_list.transpose(2, 1, 0),
-        tile_count.T,
-        q_gain.reshape(1, row_width),
-        k_gain.reshape(1, row_width),
-        query,
-        key_in,
-        value,
+        *(
+            pltpu.with_memory_space_constraint(operand, pltpu.HBM)
+            for operand in (
+                tile_list.transpose(2, 1, 0),
+                tile_count.T,
+                q_gain.reshape(1, row_width),
+                k_gain.reshape(1, row_width),
+                query,
+                key_in,
+                value,
+            )
+        )
     )
 
 

time: 100 us -> 99 us (0.990)
  local copies, waits for them, and re-layouts: 2.29 us -> 0.97 us
    unnamed x1, local copies, waits for them, and re-layouts: 2.29 us -> 0.97 us
where the time goes in v3:
time: 99 us; the launch traced here: 98.8 us
  Pallas kernels  97.9 us (99%)
    pallas_call x1, Pallas kernels, fused(): pl.pallas_call(functools.partial(attention_kernel, n, heads_dev, slot_cou...  97.9 us

profile of v3, /device:TPU:0, one launch (start us, length us, event | category | flops | bytes accessed | tf_op | source)
XLA Modules:
  0.0 98.8 jit_solution(15082290938738293387)
XLA Ops:
  0.0 97.9 %shard_map.73 = bf16[128,4096]{1,0:T(8,128)(2,1)S(1)} custom-call(s32[3,16,32]{2,1,0:T(8,128)} %bitcast.4, s32[16,32]{1,0:T(8,128)} %bitcast.7, f32[1,4096]{1,0:T(1,128)} %bitcast.5, f32[1,4096]{1,0:T(1,128)} %bitcast.6, bf16[128,4096]{1,0:T(8,128)(2,1)} %q_hbm.1, bf16[128,4096]{1,0:T(8,128)(2,1)} %k_hbm.1, bf16[128,4096]{1,0:T(8,128)(2,1)} %v_hbm.1), custom_call_target="tpu_custom_call" | custom-call | flops 805306368 | bytes 4194304 | tf_op jit(solution)/shard_map/pallas_call | solution.py:247
  97.9 1.0 copy.9

commit v4 on v3

--- a/solution.py
+++ b/solution.py
@@ -76,16 +76,19 @@
         return lax.rem(me + 1 + lax.rem(n // 2 - 1 + i, n - 1), n)
 
     def v_columns(head):
-        return v_hbm.at[:, pl.ds(pl.multiple_of(head * HEAD_DIM, HEAD_DIM), HEAD_DIM)]
+        return v_hbm.at[:, pl.ds(pl.multiple_of(head * HEAD_DIM, HEAD_DIM), heads_dev * HEAD_DIM)]
 
     def out_columns(head):
         return out.at[:, pl.ds(pl.multiple_of(head * HEAD_DIM, HEAD_DIM), HEAD_DIM)]
 
     sources = (
-        (v_columns, v_all),
+        (v_columns, (v_all,)),
         (lambda head: q_send.at[head], q_all),
         (lambda head: k_send.at[head], k_all),
     )
+
+    def kinds(h):
+        return range(3) if h == 0 else (1, 2)
 
     def own_copy(kind, h):
         source, landing = sources[kind]
@@ -138,7 +141,7 @@
     normalise(k_in, k_gain, k_send)
     spread(2, 0)
     for h in range(1, heads_dev):
-        for kind in range(3):
+        for kind in kinds(h):
             spread(kind, h)
     loads[4].wait()
     loads[5].wait()
@@ -175,7 +178,7 @@
             tile = list_smem[slot, block, me * heads_dev + h]
             product = jnp.dot(
                 weights[slot].astype(jnp.bfloat16),
-                v_all[h][tile],
+                v_all[tile, :, h * HEAD_DIM : (h + 1) * HEAD_DIM],
                 preferred_element_type=jnp.float32,
             )
             total = product if total is None else total + product
@@ -198,7 +201,7 @@
 
     last = heads_dev - 1
     for h in range(heads_dev):
-        for kind in range(3):
+        for kind in kinds(h):
             own_copy(kind, h).wait()
             landed(sources[kind][1][h], recv_sem.at[kind, h])
 
@@ -213,7 +216,7 @@
         o_send[h, me] = attend(h, me)
         kept(h).start()
         if h == last - 1:
-            for kind in range(3):
+            for kind in kinds(last):
                 landed(sources[kind][1][last], send_sem.at[kind, last])
 
             def give_back(i, carry):
@@ -228,7 +231,7 @@
         landed(o_send.at[h], back_recv_sem.at[h])
         landed(o_send.at[h], back_send_sem.at[h])
         if h < last or last == 0:
-            for kind in range(3):
+            for kind in kinds(h):
                 landed(sources[kind][1][h], send_sem.at[kind, h])
 
 
@@ -260,7 +263,7 @@
             pltpu.VMEM((head_count, BLOCK, HEAD_DIM), jnp.bfloat16),
             landing,
             landing,
-            landing,
+            pltpu.VMEM((n, BLOCK, heads_dev * HEAD_DIM), jnp.bfloat16),
             pltpu.VMEM((heads_dev, n, BLOCK, HEAD_DIM), jnp.bfloat16),
             pltpu.SemaphoreType.DMA((6,)),
             pltpu.SemaphoreType.DMA((4, heads_dev)),

time: 99 us -> 99.2 us (level)
  no operation moved by 1% of the time
where the time goes in v4:
time: 99.2 us; the launch traced here: 99.1 us
  Pallas kernels  98.1 us (99%)
    pallas_call x1, Pallas kernels, fused(): pl.pallas_call(functools.partial(attention_kernel, n, heads_dev, slot_cou...  98.1 us

profile of v4, /device:TPU:0, one launch (start us, length us, event | category | flops | bytes accessed | tf_op | source)
XLA Modules:
  0.0 99.1 jit_solution(6459318272550126671)
XLA Ops:
  0.0 98.1 %shard_map.73 = bf16[128,4096]{1,0:T(8,128)(2,1)S(1)} custom-call(s32[3,16,32]{2,1,0:T(8,128)} %bitcast.4, s32[16,32]{1,0:T(8,128)} %bitcast.7, f32[1,4096]{1,0:T(1,128)} %bitcast.5, f32[1,4096]{1,0:T(1,128)} %bitcast.6, bf16[128,4096]{1,0:T(8,128)(2,1)} %q_hbm.1, bf16[128,4096]{1,0:T(8,128)(2,1)} %k_hbm.1, bf16[128,4096]{1,0:T(8,128)(2,1)} %v_hbm.1), custom_call_target="tpu_custom_call" | custom-call | flops 805306368 | bytes 4194304 | tf_op jit(solution)/shard_map/pallas_call | solution.py:250
  98.1 1.0 copy.9
